TPU v7x, 32 devices: a whole 2x2x4 slice. The times are simulated.
32 devices in a mesh: cell: 8 (over z, y), stn: 4 (over x, core).
Axes of the slice: x: 2, y: 2, z: 4, core: 2. Of those that a mesh axis runs over, the one named last changes fastest.
Arguments:
- cell_points: float32 [3, 8192], P(None, 'cell'), may hold values from 0 to 1
- magnetization: float32 [3, 8192], P(None, 'cell'), may hold values from -6 to 6
- cell_level: int32 [8192], P('cell'), may hold values from 0 to 2
- suscept: float32 [8192], P('cell'), may hold values from 0.2 to 2
- inducing: float32 [3], replicated, may hold values from -4 to 4
- stations: float32 [3, 4096], P(None, 'stn'), may hold values from 0 to 2, as said below
Outputs:
- updated: float32 [3, 8192], P(None, ('cell', 'stn'))
- predictions: float32 [4096], P(('stn', 'cell'))
Inputs may be any that keep to these rules, and one draw needn't show every extreme that they name: `stations`: the first two coordinates lie in the unit square; the third is 1 plus 0.5 to 2 times 8192 ** (-1/3).
All inputs are finite; a program needn't handle non-finite values.
Results may differ from a plain program's by a relative error of at most 0.0003.
Values sent between devices are 32-bit elements; how exact they have to be, the bound alone decides.
A program may use at most 64 MiB of HBM per device.

v0:
```python
import math
import jax
import jax.numpy as jnp
from jax import lax
from jax.sharding import PartitionSpec as P

INV_FOUR_PI = 0.25 / math.pi


def block_width(targets, sources):
    ceiling = max(256, (1 << 20) // targets)
    ceiling = 1 << ceiling.bit_length() - 1
    return math.gcd(sources, ceiling)


def pair_field(points, source_piece):
    delta_x = points[0][:, None] - source_piece[0][None, :]
    delta_y = points[1][:, None] - source_piece[1][None, :]
    delta_z = points[2][:, None] - source_piece[2][None, :]
    soften = source_piece[6][None, :]
    radius_sq = delta_x * delta_x + delta_y * delta_y + delta_z * delta_z + soften * soften
    inverse = lax.rsqrt(radius_sq)
    inverse_sq = inverse * inverse
    weight = INV_FOUR_PI * soften * soften * soften * inverse_sq * inverse
    projection = (
        3.0
        * (
            delta_x * source_piece[3][None, :]
            + delta_y * source_piece[4][None, :]
            + delta_z * source_piece[5][None, :]
        )
        * inverse_sq
    )
    field_x = jnp.sum(weight * (projection * delta_x - source_piece[3][None, :]), axis=1)
    field_y = jnp.sum(weight * (projection * delta_y - source_piece[4][None, :]), axis=1)
    field_z = jnp.sum(weight * (projection * delta_z - source_piece[5][None, :]), axis=1)
    return jnp.stack([field_x, field_y, field_z], 0)


def source_field(points, sources):
    number = sources.shape[1]
    blockw = block_width(points.shape[1], number)
    groups = sources.reshape(7, number // blockw, blockw).transpose(1, 0, 2)

    def advance(summed, source_piece):
        return (summed + pair_field(points, source_piece), None)

    result, unused = lax.scan(advance, jnp.zeros((3, points.shape[1]), jnp.float32), groups)
    return result


def shards(cell_points, magnetization, cell_level, suscept, inducing, stations):
    cycle_size = lax.axis_size("cell")
    section = lax.axis_size("stn")
    block_cells = cell_points.shape[1]
    spacing = float(block_cells * cycle_size * section // section) ** (-1.0 / 3.0)
    size_h = spacing * jnp.power(0.5, cell_level.astype(jnp.float32))
    packed = jnp.concatenate([cell_points, magnetization, size_h[None, :]], 0)
    owned = block_cells // section
    offset = lax.axis_index("stn") * owned
    targets = lax.dynamic_slice_in_dim(cell_points, offset, owned, 1)
    demag = source_field(targets, lax.all_gather(packed, "cell", axis=1, tiled=True))
    own_suscept = lax.dynamic_slice_in_dim(suscept, offset, owned, 0)
    updated = own_suscept[None, :] * (inducing[:, None] + demag)
    block_mag = lax.all_gather(updated, "stn", axis=1, tiled=True)
    moved = jnp.concatenate([cell_points, block_mag, size_h[None, :]], 0)
    field = source_field(stations, moved)
    predictions = lax.psum_scatter(
        jnp.sum(inducing[:, None] * field, axis=0), "cell", scatter_dimension=0, tiled=True
    )
    return (updated, predictions)


def solution(mesh):
    placed = (P(None, "cell"), P(None, "cell"), P("cell"), P("cell"), P(), P(None, "stn"))
    return jax.shard_map(
        shards,
        mesh=mesh,
        in_specs=placed,
        out_specs=(P(None, ("cell", "stn")), P(("stn", "cell"))),
        check_vma=False,
    )
```

profile of v0, /device:TPU:0, one launch (start us, length us, event | category | flops | bytes accessed | tf_op | source)
XLA Modules:
  0.0 82.9 jit_solution(14544340827631167878)
XLA Ops:
  0.6 0.7 constant_dynamic-slice_fusion.7
  1.3 0.7 multiply_multiply_fusion.3
  2.0 0.8 pad_maximum_fusion
  2.8 32.5 %all_gather.6 = f32[7,8192]{1,0:T(8,128)S(1)} all-gather(f32[7,1024]{1,0:T(8,128)S(1)} %pad_maximum_fusion), channel_id=1, replica_groups=mesh['cell'=8,'stn'=4] {'cell'}, dimensions={1}, use_global_device_ids=true | all-gather | bytes 258048 | tf_op jit(solution)/shard_map/all_gather | solution.py:62
  35.3 0.0 copy-start.3
  35.3 11.8 %while.3 = (s32[]{:T(128)}, f32[3,256]{1,0:T(4,128)S(1)}, f32[2,7,4096]{2,1,0:T(8,128)S(1)}, f32[3,256]{1,0:T(4,128)S(1)}, s32[]{:T(128)}, /*index=5*/s32[]{:T(128)}, s32[]{}, s32[]{}, s32[]{}, s32[]{}, /*index=10*/s32[]{}, s32[]{}) while((s32[]{:T(128)}, f32[3,256]{1,0:T(4,128)S(1)}, f32[2,7,4096]{2,1,0:T(8,128)S(1)}, ...), condition=%wide.region_4.5_spmd.clone, body=%wide.region_0.4_spmd.clone.sunk | while | flops 32524552 | bytes 431331 | solution.py:48
  35.3 0.1 constant_dynamic-slice_fusion.9
  35.5 5.7 %fusion.44 = (f32[256]{0:T(256)S(1)}, f32[256]{0:T(256)S(1)}, f32[256]{0:T(256)S(1)}) fusion(f32[4096]{0:T(1024)S(1)} %bitcast.60, f32[4096]{0:T(1024)S(1)} %bitcast.62, f32[256]{0:T(256)S(1)} %bitcast.69, f32[4096]{0:T(1024)S(1)} %get-tuple-element.134, f32[4096]{0:T(1024)S(1)} %bitcast.63, f32[4096]{0:T(1024)S(1)} %bitcast.61, f32[256]{0:T(256)S(1)} %bitcast.68, ...), kind=kLoop, calls=%fused_computation.19.clone.1 | loop fusion | flops 32505088 | bytes 137216 | tf_op jit(solution)/shard_map/while/body/eval_jaxpr/reduce_sum | solution.py:34
  41.2 0.1 constant_dynamic-slice_fusion.9
  41.4 5.7 %fusion.44 = (f32[256]{0:T(256)S(1)}, f32[256]{0:T(256)S(1)}, f32[256]{0:T(256)S(1)}) fusion(f32[4096]{0:T(1024)S(1)} %bitcast.60, f32[4096]{0:T(1024)S(1)} %bitcast.62, f32[256]{0:T(256)S(1)} %bitcast.69, f32[4096]{0:T(1024)S(1)} %get-tuple-element.134, f32[4096]{0:T(1024)S(1)} %bitcast.63, f32[4096]{0:T(1024)S(1)} %bitcast.61, f32[256]{0:T(256)S(1)} %bitcast.68, ...), kind=kLoop, calls=%fused_computation.19.clone.1 | loop fusion | flops 32505088 | bytes 137216 | tf_op jit(solution)/shard_map/while/body/eval_jaxpr/reduce_sum | solution.py:34
  47.2 0.8 dynamic_slice.13
  47.9 0.0 copy-done.3
  47.9 0.1 add_multiply_fusion
  48.0 5.2 %all_gather.7 = f32[3,1024]{1,0:T(4,128)S(1)} all-gather(f32[3,256]{1,0:T(4,128)S(1)} %add_multiply_fusion), channel_id=1, replica_groups=mesh['cell'=8,'stn'=4] {'stn'}, dimensions={1}, use_global_device_ids=true | all-gather | bytes 15360 | tf_op jit(solution)/shard_map/all_gather | solution.py:65
  53.2 0.0 copy-done.2
  53.2 0.0 copy-done
  53.2 0.0 copy-start.4
  53.3 6.2 %fusion.27 = (f32[1024]{0:T(1024)S(1)}, f32[1024]{0:T(1024)S(1)}, f32[1024]{0:T(1024)S(1)}) fusion(f32[1024]{0:T(1024)S(1)} %bitcast.73, f32[1024]{0:T(1024)S(1)} %bitcast.78, f32[1024]{0:T(1024)S(1)} %bitcast.75, f32[1024]{0:T(1024)S(1)} %get-tuple-element.88, f32[1024]{0:T(1024)S(1)} %bitcast.72, f32[1024]{0:T(1024)S(1)} %bitcast.79, ...), kind=kLoop, calls=%fused_computation.55 | loop fusion | flops 32502784 | bytes 57344 | tf_op jit(solution)/shard_map/while/body/eval_jaxpr/reduce_sum | solution.py:34
  59.5 0.0 copy-done.1
  59.5 0.1 fusion.34
  59.6 21.4 %all-reduce = f32[1024]{0:T(1024)S(1)} all-reduce(f32[1024]{0:T(1024)S(1)} %fusion.34), channel_id=2, replica_groups=mesh['cell'=8,'stn'=4] {'cell'}, use_global_device_ids=true, to_apply=%region_9.10.clone | all-reduce | flops 1024 | bytes 8192
  81.0 0.0 copy-done.4
  81.0 0.6 dynamic-slice.1
  82.3 0.6 dynamic-slice.2
  (13 shorter events, 0.1 us)
Async XLA Ops:
  35.3 12.6 %copy-start.3 = (f32[3]{0:T(128)S(1)}, f32[3]{0:T(128)}, u32[]{:S(2)}) copy-start(f32[3]{0:T(128)} %param.12) | copy-start | bytes 40
  35.3 17.9 %copy-start.2 = (f32[3,1024]{1,0:T(4,128)S(1)}, f32[3,1024]{1,0:T(4,128)}, u32[]{:S(2)}) copy-start(f32[3,1024]{1,0:T(4,128)} %param.13) | copy-start | bytes 36868
  35.3 17.9 %copy-start = (f32[3,1024]{1,0:T(4,128)S(1)}, f32[3,1024]{1,0:T(4,128)}, u32[]{:S(2)}) copy-start(f32[3,1024]{1,0:T(4,128)} %param.8) | copy-start | bytes 36868
  48.0 11.5 %copy-start.1 = (f32[3,256]{1,0:T(4,128)}, f32[3,256]{1,0:T(4,128)S(1)}, u32[]{:S(2)}) copy-start(f32[3,256]{1,0:T(4,128)S(1)} %add_multiply_fusion) | copy-start | bytes 9220
  53.2 27.8 %copy-start.4 = (u32[32]{0:T(128)S(1)}, u32[32]{0:T(128)}, u32[]{:S(2)}) copy-start(u32[32]{0:T(128)} %constant.48) | copy-start | bytes 388
where the time goes:
time: 83.3 us; the launch traced here: 82.9 us
  blocking collectives  59.1 us (71%)
  other arithmetic  19.4 us (23%)
  local copies, waits for them, and re-layouts  2.93 us (4%)
  between operations  1.37 us (2%)
    all_gather x1, blocking collectives, shards(): lax.all_gather(packed, 'cell', axis=1, tiled=True)  32.5 us
    unnamed x1, blocking collectives  21.4 us
    reduce_sum x3, other arithmetic, pair_field(): jnp.sum(weight * (projection * delta_x - source_piece[3][None, :]), axis=1)  17.7 us
    all_gather x1, blocking collectives, shards(): block_mag = lax.all_gather(updated, 'stn', axis=1, tiled=True)  5.17 us

commit v1 on v0

--- a/solution.py
+++ b/solution.py
@@ -5,6 +5,18 @@
 from jax.sharding import PartitionSpec as P
 
 INV_FOUR_PI = 0.25 / math.pi
+
+
+def gather_by_bits(array, axis, dim):
+    ways, here = (lax.axis_size(axis), lax.axis_index(axis))
+    grown, reach = (array, 1)
+    while reach < ways:
+        theirs = lax.ppermute(grown, axis, [(d, d ^ reach) for d in range(ways)])
+        mine_first = jnp.concatenate([grown, theirs], axis=dim)
+        theirs_first = jnp.concatenate([theirs, grown], axis=dim)
+        grown = jnp.where(here & reach == 0, mine_first, theirs_first)
+        reach = 2 * reach
+    return grown
 
 
 def block_width(targets, sources):
@@ -59,7 +71,7 @@
     owned = block_cells // section
     offset = lax.axis_index("stn") * owned
     targets = lax.dynamic_slice_in_dim(cell_points, offset, owned, 1)
-    demag = source_field(targets, lax.all_gather(packed, "cell", axis=1, tiled=True))
+    demag = source_field(targets, gather_by_bits(packed, "cell", 1))
     own_suscept = lax.dynamic_slice_in_dim(suscept, offset, owned, 0)
     updated = own_suscept[None, :] * (inducing[:, None] + demag)
     block_mag = lax.all_gather(updated, "stn", axis=1, tiled=True)

time: 83.3 us -> 67.8 us (0.81)
  blocking collectives: 59.1 us -> 25.7 us
  starting transfers between devices: 0 us -> 7.33 us
  waiting for transfers between devices: 0 us -> 6.91 us
  local copies, waits for them, and re-layouts: 2.93 us -> 5.23 us
    all_gather x1 -> x0, blocking collectives: 32.5 us -> none  [shards(): lax.all_gather(packed, 'cell', axis=1, tiled=True)]
    ppermute x0 -> x3, starting transfers between devices: none -> 7.33 us  [gather_by_bits(): theirs = lax.ppermute(grown, axis, [(d, d ^ reach) for d in range(ways)])]
    ppermute x0 -> x3, waiting for transfers between devices: none -> 6.91 us  [gather_by_bits(): theirs = lax.ppermute(grown, axis, [(d, d ^ reach) for d in range(ways)])]
    slice x6, local copies, waits for them, and re-layouts: 0.27 us -> 1.93 us  [pair_field(): delta_y = points[1][:, None] - source_piece[1][None, :]]
    unnamed x1, blocking collectives: 21.4 us -> 20.6 us
    select_n x0 -> x3, other arithmetic: none -> 0.86 us  [gather_by_bits(): grown = jnp.where(here & reach == 0, mine_first, theirs_first)]
    unnamed x12 -> x6, local copies, waits for them, and re-layouts: 1.19 us -> 1.83 us
  transfers between devices with their start and end apart: 0 -> 3, of which waited for: 0 -> 2; matrix products, arithmetic and copies ran while one was open for 0% -> 7% of each run, Pallas kernels for 0% -> 0%
where the time goes in v1:
time: 67.8 us; the launch traced here: 66.9 us
  blocking collectives  25.7 us (38%)
  other arithmetic  20.2 us (30%)
  starting transfers between devices  7.33 us (11%)
  waiting for transfers between devices  6.91 us (10%)
  local copies, waits for them, and re-layouts  5.23 us (8%)
  between operations  1.39 us (2%)
    unnamed x1, blocking collectives  20.6 us
    reduce_sum x3, other arithmetic, pair_field(): jnp.sum(weight * (projection * delta_x - source_piece[3][None, :]), axis=1)  17.7 us
    ppermute x3, starting transfers between devices, gather_by_bits(): theirs = lax.ppermute(grown, axis, [(d, d ^ reach) for d in range(ways)])  7.33 us
    ppermute x3, waiting for transfers between devices, gather_by_bits(): theirs = lax.ppermute(grown, axis, [(d, d ^ reach) for d in range(ways)])  6.91 us
    all_gather x1, blocking collectives, shards(): block_mag = lax.all_gather(updated, 'stn', axis=1, tiled=True)  5.17 us
    slice x6, local copies, waits for them, and re-layouts, pair_field(): delta_y = points[1][:, None] - source_piece[1][None, :]  1.93 us
    unnamed x6, local copies, waits for them, and re-layouts  1.83 us
  transfers between devices with their start and end apart: 3, of which 2 were waited for; matrix products, arithmetic and copies ran while one was open for 7% of the time, Pallas kernels for 0%

profile of v1, /device:TPU:0, one launch (start us, length us, event | category | flops | bytes accessed | tf_op | source)
XLA Modules:
  0.0 66.9 jit_solution(12091973498748408185)
XLA Ops:
  0.6 0.7 %multiply_multiply_fusion.3 = (f32[1024]{0:T(1024)S(1)}, f32[1024]{0:T(1024)S(1)}, f32[1024]{0:T(1024)S(1)}) fusion(s32[1024]{0:T(1024)} %param.10), kind=kLoop, calls=%fused_computation.71 | loop fusion | flops 6144 | bytes 16384 | tf_op jit(solution)/shard_map/while/body/eval_jaxpr/mul | solution.py:36
  1.3 0.8 %pad_maximum_fusion = f32[7,1024]{1,0:T(8,128)S(1)} fusion(f32[1,1024]{1,0:T(1,128)S(1)} %bitcast.68, f32[3,1024]{1,0:T(4,128)} %param.9, f32[3,1024]{1,0:T(4,128)} %param.8), kind=kLoop, calls=%fused_computation.68 | loop fusion | flops 14336 | bytes 57344 | tf_op jit(solution)/shard_map/concatenate | solution.py:70
  2.1 3.0 %collective-permute-start = (f32[7,1024]{1,0:T(8,128)S(1)}, f32[7,1024]{1,0:T(8,128)S(1)}, u32[]{:S(2)}, u32[]{:S(2)}) collective-permute-start(f32[7,1024]{1,0:T(8,128)S(1)} %pad_maximum_fusion), channel_id=1, source_target_pairs={{0,4},{4,0},{8,12},{12,8},{16,20},{20,16},{24,28},{28,24},{1,5},{5... | collective-permute-start | bytes 86024 | tf_op jit(solution)/shard_map/ppermute | solution.py:14
  5.1 0.8 %fusion.40 = (f32[1,1024]{1,0:T(1,128)S(1)}, f32[1,1024]{1,0:T(1,128)S(1)}, f32[1,1024]{1,0:T(1,128)S(1)}) fusion(f32[3,1024]{1,0:T(4,128)} %param.8), kind=kLoop, calls=%fused_computation.79 | loop fusion | bytes 24576 | tf_op jit(solution)/shard_map/while/body/eval_jaxpr/slice | solution.py:30
  6.0 0.8 %fusion.39 = (f32[1,1024]{1,0:T(1,128)S(1)}, f32[1,1024]{1,0:T(1,128)S(1)}, f32[1,1024]{1,0:T(1,128)S(1)}) fusion(f32[3,1024]{1,0:T(4,128)} %param.13), kind=kLoop, calls=%fused_computation.78 | loop fusion | bytes 24576 | tf_op jit(solution)/shard_map/while/body/eval_jaxpr/slice | solution.py:30
  6.8 0.8 %dynamic_slice.13 = f32[256]{0:T(256)S(1)} dynamic-slice(f32[1024]{0:T(1024)} %param.11, s32[]{:T(128)S(6)} %select_n.44), dynamic_slice_sizes={256} | dynamic-slice | bytes 2052 | tf_op jit(solution)/shard_map/dynamic_slice | solution.py:75
  7.6 1.2 %dynamic-slice.1 = u32[1]{0:T(128)} dynamic-slice(u32[32]{0:T(128)} %constant.59, u32[]{:T(128)S(6)} %add.90), dynamic_slice_sizes={1} | dynamic-slice | bytes 12
  9.5 0.8 %maximum_select_fusion.3 = f32[7,2048]{1,0:T(8,128)S(1)} fusion(f32[7,1024]{1,0:T(8,128)S(1)} %collective-permute-done, f32[1,1024]{1,0:T(1,128)S(1)} %bitcast.69, f32[3,1024]{1,0:T(4,128)} %param.9, f32[3,1024]{1,0:T(4,128)} %param.8, pred[]{:T(512)S(6)} %eq.11), kind=kLoop, calls=%fused_computation.67 | loop fusion | flops 100352 | bytes 114689 | tf_op jit(solution)/shard_map/jit(_where)/select_n | solution.py:17
  10.3 1.6 %collective-permute-start.1 = (f32[7,2048]{1,0:T(8,128)S(1)}, f32[7,2048]{1,0:T(8,128)S(1)}, u32[]{:S(2)}, u32[]{:S(2)}) collective-permute-start(f32[7,2048]{1,0:T(8,128)S(1)} %maximum_select_fusion.3), channel_id=1, source_target_pairs={{0,8},{4,12},{8,0},{12,4},{16,24},{20,28},{24,16},{28,20},{1,9},{5... | collective-permute-start | bytes 172040 | tf_op jit(solution)/shard_map/ppermute | solution.py:14
  12.0 0.7 %constant_dynamic-slice_fusion.7 = f32[3,256]{1,0:T(4,128)S(1)} fusion(f32[3,1024]{1,0:T(4,128)} %param.8, s32[]{:T(128)S(6)} %select_n.44), kind=kLoop, calls=%fused_computation.76 | loop fusion | bytes 6148 | tf_op jit(solution)/shard_map/dynamic_slice | solution.py:73
  12.7 2.0 %collective-permute-done.1 = f32[7,2048]{1,0:T(8,128)S(1)} collective-permute-done((f32[7,2048]{1,0:T(8,128)S(1)}, f32[7,2048]{1,0:T(8,128)S(1)}, u32[]{:S(2)}, u32[]{:S(2)}) %collective-permute-start.1) | collective-permute-done | bytes 57376 | tf_op jit(solution)/shard_map/ppermute | solution.py:14
  14.7 2.7 %collective-permute-start.2 = (f32[7,4096]{1,0:T(8,128)S(1)}, f32[7,4096]{1,0:T(8,128)S(1)}, u32[]{:S(2)}, u32[]{:S(2)}) collective-permute-start(f32[7,4096]{1,0:T(8,128)S(1)} %maximum_select_fusion.2), channel_id=1, source_target_pairs={{0,16},{4,20},{8,24},{12,28},{16,0},{20,4},{24,8},{28,12},{1,17},{... | collective-permute-start | bytes 344072 | tf_op jit(solution)/shard_map/ppermute | solution.py:14
  17.4 4.9 %collective-permute-done.2 = f32[7,4096]{1,0:T(8,128)S(1)} collective-permute-done((f32[7,4096]{1,0:T(8,128)S(1)}, f32[7,4096]{1,0:T(8,128)S(1)}, u32[]{:S(2)}, u32[]{:S(2)}) %collective-permute-start.2) | collective-permute-done | bytes 114720 | tf_op jit(solution)/shard_map/ppermute | solution.py:14
  22.3 11.8 %while.3 = (s32[]{:T(128)}, f32[3,256]{1,0:T(4,128)S(1)}, f32[2,7,4096]{2,1,0:T(8,128)S(1)}, f32[3,256]{1,0:T(4,128)S(1)}, s32[]{:T(128)}, /*index=5*/s32[]{:T(128)}, s32[]{}, s32[]{}, s32[]{}, s32[]{}, /*index=10*/s32[]{}, s32[]{}) while((s32[]{:T(128)}, f32[3,256]{1,0:T(4,128)S(1)}, f32[2,7,4096]{2,1,0:T(8,128)S(1)}, ...), condition=%wide.region_4.5_spmd.clone, body=%wide.region_0.4_spmd.clone.sunk | while | flops 32524552 | bytes 431331 | solution.py:60
  22.3 0.1 constant_dynamic-slice_fusion.9
  22.5 5.7 %fusion.45 = (f32[256]{0:T(256)S(1)}, f32[256]{0:T(256)S(1)}, f32[256]{0:T(256)S(1)}) fusion(f32[4096]{0:T(1024)S(1)} %bitcast.62, f32[4096]{0:T(1024)S(1)} %bitcast.64, f32[256]{0:T(256)S(1)} %bitcast.75, f32[4096]{0:T(1024)S(1)} %get-tuple-element.134, f32[4096]{0:T(1024)S(1)} %bitcast.65, f32[4096]{0:T(1024)S(1)} %bitcast.63, f32[256]{0:T(256)S(1)} %bitcast.74, ...), kind=kLoop, calls=%fused_computation.19.clone.1 | loop fusion | flops 32505088 | bytes 137216 | tf_op jit(solution)/shard_map/while/body/eval_jaxpr/reduce_sum | solution.py:46
  28.2 0.1 constant_dynamic-slice_fusion.9
  28.4 5.7 %fusion.45 = (f32[256]{0:T(256)S(1)}, f32[256]{0:T(256)S(1)}, f32[256]{0:T(256)S(1)}) fusion(f32[4096]{0:T(1024)S(1)} %bitcast.62, f32[4096]{0:T(1024)S(1)} %bitcast.64, f32[256]{0:T(256)S(1)} %bitcast.75, f32[4096]{0:T(1024)S(1)} %get-tuple-element.134, f32[4096]{0:T(1024)S(1)} %bitcast.65, f32[4096]{0:T(1024)S(1)} %bitcast.63, f32[256]{0:T(256)S(1)} %bitcast.74, ...), kind=kLoop, calls=%fused_computation.19.clone.1 | loop fusion | flops 32505088 | bytes 137216 | tf_op jit(solution)/shard_map/while/body/eval_jaxpr/reduce_sum | solution.py:46
  34.2 0.1 add_multiply_fusion
  34.2 5.2 %all_gather.3 = f32[3,1024]{1,0:T(4,128)S(1)} all-gather(f32[3,256]{1,0:T(4,128)S(1)} %add_multiply_fusion), channel_id=1, replica_groups=mesh['cell'=8,'stn'=4] {'stn'}, dimensions={1}, use_global_device_ids=true | all-gather | bytes 15360 | tf_op jit(solution)/shard_map/all_gather | solution.py:77
  39.4 6.2 %fusion.27 = (f32[1024]{0:T(1024)S(1)}, f32[1024]{0:T(1024)S(1)}, f32[1024]{0:T(1024)S(1)}) fusion(f32[1024]{0:T(1024)S(1)} %bitcast.84, f32[1024]{0:T(1024)S(1)} %bitcast.77, f32[1024]{0:T(1024)S(1)} %bitcast.80, f32[1024]{0:T(1024)S(1)} %get-tuple-element.88, f32[1024]{0:T(1024)S(1)} %bitcast.83, f32[1024]{0:T(1024)S(1)} %bitcast.78, ...), kind=kLoop, calls=%fused_computation.55 | loop fusion | flops 32502784 | bytes 57344 | tf_op jit(solution)/shard_map/while/body/eval_jaxpr/reduce_sum | solution.py:46
  45.7 0.1 fusion.35
  45.8 20.6 %all-reduce = f32[1024]{0:T(1024)S(1)} all-reduce(f32[1024]{0:T(1024)S(1)} %fusion.35), channel_id=2, replica_groups=mesh['cell'=8,'stn'=4] {'cell'}, use_global_device_ids=true, to_apply=%region_9.10.clone | all-reduce | flops 1024 | bytes 8192
  66.3 0.6 dynamic-slice.2
  (16 shorter events, 0.1 us)
Async XLA Ops:
  2.1 7.4 %collective-permute-start = (f32[7,1024]{1,0:T(8,128)S(1)}, f32[7,1024]{1,0:T(8,128)S(1)}, u32[]{:S(2)}, u32[]{:S(2)}) collective-permute-start(f32[7,1024]{1,0:T(8,128)S(1)} %pad_maximum_fusion), channel_id=1, source_target_pairs={{0,4},{4,0},{8,12},{12,8},{16,20},{20,16},{24,28},{28,24},{1,5},{5... | collective-permute-start | bytes 86024 | tf_op jit(solution)/shard_map/ppermute | solution.py:14
  10.3 4.3 %collective-permute-start.1 = (f32[7,2048]{1,0:T(8,128)S(1)}, f32[7,2048]{1,0:T(8,128)S(1)}, u32[]{:S(2)}, u32[]{:S(2)}) collective-permute-start(f32[7,2048]{1,0:T(8,128)S(1)} %maximum_select_fusion.3), channel_id=1, source_target_pairs={{0,8},{4,12},{8,0},{12,4},{16,24},{20,28},{24,16},{28,20},{1,9},{5... | collective-permute-start | bytes 172040 | tf_op jit(solution)/shard_map/ppermute | solution.py:14
  14.7 7.6 %collective-permute-start.2 = (f32[7,4096]{1,0:T(8,128)S(1)}, f32[7,4096]{1,0:T(8,128)S(1)}, u32[]{:S(2)}, u32[]{:S(2)}) collective-permute-start(f32[7,4096]{1,0:T(8,128)S(1)} %maximum_select_fusion.2), channel_id=1, source_target_pairs={{0,16},{4,20},{8,24},{12,28},{16,0},{20,4},{24,8},{28,12},{1,17},{... | collective-permute-start | bytes 344072 | tf_op jit(solution)/shard_map/ppermute | solution.py:14
  22.3 11.9 %copy-start.1 = (f32[3]{0:T(128)S(1)}, f32[3]{0:T(128)}, u32[]{:S(2)}) copy-start(f32[3]{0:T(128)} %param.12) | copy-start | bytes 40
  34.2 11.4 %copy-start = (f32[3,256]{1,0:T(4,128)}, f32[3,256]{1,0:T(4,128)S(1)}, u32[]{:S(2)}) copy-start(f32[3,256]{1,0:T(4,128)S(1)} %add_multiply_fusion) | copy-start | bytes 9220
